TPU v7x, 32 devices: a whole 2x2x4 slice. The times are simulated.
32 devices in a mesh: tm: 4 (over z), space: 8 (over y, x, core).
Axes of the slice: x: 2, y: 2, z: 4, core: 2. Of those that a mesh axis runs over, the one named last changes fastest.
Arguments:
- queries: bfloat16 [4096, 2560], P(('tm', 'space')), may hold values from -6 to 6
- keys: bfloat16 [4096, 2560], P(('tm', 'space')), may hold values from -6 to 6
- values: bfloat16 [4096, 2560], P(('tm', 'space')), may hold values from -6 to 6
- grad_out: bfloat16 [4096, 2560], P(('tm', 'space')), may hold values from -6 to 6
- saved_state: bfloat16 [4, 20, 128, 128], P('tm', None, 'space'), may hold values from -0.3984375 to 0.3984375
Outputs:
- grad_q: bfloat16 [4096, 2560], P(('tm', 'space'))
- grad_k: bfloat16 [4096, 2560], P(('tm', 'space'))
- grad_v: bfloat16 [4096, 2560], P(('tm', 'space'))
All inputs are finite; a program needn't handle non-finite values.
Results may differ from a plain program's by a relative error of at most 0.0049.
Values may be sent and summed in bfloat16 or wider, within the bound.
No kernel may reach another device: no remote copies, remote signals or barrier semaphores. Data moves between devices by JAX's collectives and lax.ppermute only.
A program may use at most 64 MiB of HBM per device.

v0:
```python
import functools
import math

import jax
import jax.numpy as jnp
from jax import lax
from jax.experimental import pallas as pl
from jax.experimental.pallas import tpu as pltpu
from jax.sharding import PartitionSpec as P

CONTRACT_ROWS = (((0,), (0,)), ((), ()))
CONTRACT_COLS = (((1,), (1,)), ((), ()))
VMEM_BYTES = 16 * 1024 * 1024
ANYWHERE = pl.BlockSpec(memory_space=pl.ANY)
IN_VMEM = pl.BlockSpec(memory_space=pltpu.VMEM)


def power_of_two(count):
    return count & (count - 1) == 0


def partner(group, hop, groups):
    if power_of_two(groups):
        return group ^ hop
    return (group + hop) % groups


def source(group, hop, groups):
    if power_of_two(groups):
        return group ^ hop
    return (group - hop + groups) % groups


def cost(flops, *arrays):
    moved = sum(array.size * array.dtype.itemsize for array in arrays)
    return pl.CostEstimate(flops=flops, bytes_accessed=moved, transcendentals=0)


def after(value, earlier):
    return lax.optimization_barrier((value, earlier))[0]


def place_on_space(lanes):
    index = lax.axis_index("space")
    return lax.div(index, lanes), lax.rem(index, lanes)


def swap_lanes(value, lanes, groups):
    pairs = [(g * lanes + c, g * lanes + 1 - c) for g in range(groups) for c in range(lanes)]
    return lax.ppermute(value, "space", pairs)


def hop_groups(value, hop, lanes, groups):
    pairs = [
        (g * lanes + c, partner(g, hop, groups) * lanes + c)
        for g in range(groups)
        for c in range(lanes)
    ]
    return lax.ppermute(value, "space", pairs)


def gather_groups(value, waits, lanes, groups):
    if power_of_two(groups):
        for step in range(groups.bit_length() - 1):
            value = after(value, waits[min(step, len(waits) - 1)])
            value = jnp.concatenate([value, hop_groups(value, 1 << step, lanes, groups)])
        return value
    return jnp.concatenate(
        [value] + [hop_groups(value, hop, lanes, groups) for hop in range(1, groups)]
    )


def products(scale, queries, grad_out):
    return scale * lax.dot_general(
        jnp.maximum(queries, 0),
        grad_out,
        CONTRACT_ROWS,
        preferred_element_type=jnp.float32,
    )


def partial_kernel(lanes, other, scale, q_ref, o_ref, part_ref):
    span, head = part_ref.shape
    _, lane = place_on_space(lanes)
    base = (1 - lane if other else lane) * span
    for h in range(span // head):
        rows = pl.ds(h * head, head)
        cols = pl.ds(pl.multiple_of(base + h * head, head), head)
        part_ref[rows, :] = products(
            scale, q_ref[:, rows if other else cols], o_ref[:, cols]
        ).astype(part_ref.dtype)


def partial_products(queries, grad_out, head, lanes, other, scale):
    tokens, width = grad_out.shape
    span = width // lanes
    return pl.pallas_call(
        functools.partial(partial_kernel, lanes, other, scale),
        out_shape=jax.ShapeDtypeStruct((span, head), jnp.bfloat16 if other else jnp.float32),
        in_specs=[IN_VMEM, IN_VMEM],
        out_specs=IN_VMEM,
        compiler_params=pltpu.CompilerParams(vmem_limit_bytes=VMEM_BYTES),
        cost_estimate=cost(2 * tokens * span * head, queries),
        name="partial_other" if other else "partial_own",
    )(queries, grad_out)


def cut_kernel(lanes, groups, *refs):
    parts, outs = refs[:lanes], refs[lanes:]
    group, _ = place_on_space(lanes)
    rows = outs[0].shape[0]
    for hop, out_ref in enumerate(outs):
        there = pl.ds(pl.multiple_of(partner(group, hop, groups) * rows, rows), rows)
        total = parts[0][there, :]
        for part in parts[1:]:
            total = total + part[there, :].astype(jnp.float32)
        out_ref[...] = total.astype(out_ref.dtype)


def cut_by_group(parts, lanes, groups):
    span, head = parts[0].shape
    rows = span // groups
    outs = [jax.ShapeDtypeStruct((rows, head), jnp.float32)]
    outs += [jax.ShapeDtypeStruct((rows, head), jnp.bfloat16)] * (groups - 1)
    return pl.pallas_call(
        functools.partial(cut_kernel, lanes, groups),
        out_shape=outs,
        in_specs=[IN_VMEM] * lanes,
        out_specs=[IN_VMEM] * groups,
        compiler_params=pltpu.CompilerParams(vmem_limit_bytes=VMEM_BYTES),
        cost_estimate=cost(span * head, *parts),
        name="cut_by_group",
    )(*parts)


def query_kernel(lanes, q_ref, o_ref, *rest):
    sides, (dq_ref, state, sems) = rest[:lanes], rest[lanes:]
    head = state.shape[1]
    groups, _, rows, _ = sides[0].shape
    group, lane = place_on_space(lanes)
    copies = []
    for other, side in enumerate(sides):
        there = 1 - lane if other else lane
        for hop in range(groups):
            owner = source(group, hop, groups) * lanes + there
            place = pl.ds(pl.multiple_of(owner * rows, rows), rows)
            if rows % 16 == 0:
                state[:, place, :] = side[hop]
            else:
                copies.append(
                    pltpu.make_async_copy(side.at[hop], state.at[:, place, :], sems.at[other, hop])
                )
    for copy in copies:
        copy.start()
    for copy in copies:
        copy.wait()
    for h in range(state.shape[0]):
        cols = pl.ds(h * head, head)
        full = lax.dot_general(
            o_ref[:, cols], state[h], CONTRACT_COLS, preferred_element_type=jnp.float32
        )
        dq_ref[:, cols] = jnp.where(q_ref[:, cols] > 0, full, 0.0).astype(dq_ref.dtype)


def query_grads(queries, grad_out, sides):
    lanes, (groups, heads, _, head) = len(sides), sides[0].shape
    return pl.pallas_call(
        functools.partial(query_kernel, lanes),
        out_shape=jax.ShapeDtypeStruct(queries.shape, queries.dtype),
        in_specs=[IN_VMEM] * (2 + lanes),
        out_specs=IN_VMEM,
        scratch_shapes=[
            pltpu.VMEM((heads, head, head), sides[0].dtype),
            pltpu.SemaphoreType.DMA((lanes, groups)),
        ],
        compiler_params=pltpu.CompilerParams(vmem_limit_bytes=VMEM_BYTES),
        cost_estimate=cost(2 * queries.size * head, queries, queries, grad_out, *sides),
        name="query_grads",
    )(queries, grad_out, *sides)


def key_value_kernel(lanes, other, steps, k_ref, v_ref, state_ref, *rest):
    dk_hbm, dv_hbm, state, dk_buf, dv_buf, sems = rest[-6:]
    span, head = state.shape
    groups, rows, _ = state_ref.shape
    group, lane = place_on_space(lanes)
    for hop in range(groups):
        owner = source(group, hop, groups)
        state[pl.ds(pl.multiple_of(owner * rows, rows), rows), :] = state_ref[hop]
    base = (1 - lane if other else lane) * span
    part = span // steps
    copies = []
    for step in range(steps):
        for h in range(part // head):
            local = pl.ds(step * part + h * head, head)
            cols = pl.ds(pl.multiple_of(base + step * part + h * head, head), head)
            keys = k_ref[:, cols]
            grad_state = state[local, :]
            full = lax.dot_general(
                v_ref[:, cols], grad_state, CONTRACT_COLS, preferred_element_type=jnp.float32
            )
            dk_buf[:, local] = jnp.where(keys > 0, full, 0.0).astype(dk_buf.dtype)
            dv_buf[:, local] = jnp.dot(
                jnp.maximum(keys, 0), grad_state, preferred_element_type=jnp.float32
            ).astype(dv_buf.dtype)
        src = pl.ds(step * part, part)
        dst = pl.ds(pl.multiple_of(base + step * part, head), part)
        for kind, (buf, hbm) in enumerate(((dk_buf, dk_hbm), (dv_buf, dv_hbm))):
            copy = pltpu.make_async_copy(buf.at[:, src], hbm.at[:, dst], sems.at[kind, step])
            copy.start()
            copies.append(copy)
    for copy in copies:
        copy.wait()


def key_value_grads(keys, values, state, other, before, lanes):
    tokens, (groups, rows, head) = keys.shape[0], state.shape
    span = groups * rows
    steps = math.gcd(span // head, 5)
    return pl.pallas_call(
        functools.partial(key_value_kernel, lanes, other, steps),
        out_shape=(
            jax.ShapeDtypeStruct(keys.shape, keys.dtype),
            jax.ShapeDtypeStruct(values.shape, values.dtype),
        ),
        in_specs=[IN_VMEM] * 3 + [ANYWHERE] * len(before),
        out_specs=(ANYWHERE, ANYWHERE),
        scratch_shapes=[
            pltpu.VMEM((span, head), state.dtype),
            pltpu.VMEM((tokens, span), keys.dtype),
            pltpu.VMEM((tokens, span), values.dtype),
            pltpu.SemaphoreType.DMA((2, steps)),
        ],
        input_output_aliases={3 + at: at for at in range(len(before))},
        compiler_params=pltpu.CompilerParams(vmem_limit_bytes=VMEM_BYTES),
        cost_estimate=cost(4 * tokens * span * head, state, state),
        name="key_value_other" if other else "key_value_own",
    )(keys, values, state, *before)


def suffix_sum(share, blocks):
    block = lax.axis_index("tm")
    suffix = total = first = share
    if power_of_two(blocks):
        hop = 1
        while hop < blocks:
            pairs = [(b, b ^ hop) for b in range(blocks)]
            met = lax.ppermute(total.astype(jnp.bfloat16), "tm", pairs).astype(jnp.float32)
            suffix = suffix + jnp.where(block & hop == 0, met, 0.0)
            total = total + met
            first = total if hop == 1 else first
            hop *= 2
    else:
        for hop in range(1, blocks):
            pairs = [(b, b - hop) for b in range(hop, blocks)]
            later = lax.ppermute(share.astype(jnp.bfloat16), "tm", pairs)
            suffix = suffix + later.astype(jnp.float32)
    return suffix.astype(jnp.bfloat16), first


def per_device(queries, keys, values, grad_out, saved_state):
    heads, _, head = saved_state.shape[1:]
    blocks, devices = lax.axis_size("tm"), lax.axis_size("space")
    lanes = 2 if devices % 2 == 0 and heads % 2 == 0 else 1
    groups = devices // lanes
    far_first = range(groups - 1, 0, -1)
    scale = 1.0 / math.sqrt(queries.shape[0] * blocks * devices * head)

    parts = []
    if lanes > 1:
        _, lane = place_on_space(lanes)
        span = queries.shape[1] // lanes
        starts = (jnp.zeros_like(lane), (1 - lane) * span)
        cut = lax.dynamic_slice(
            queries, starts, (queries.shape[0], span), allow_negative_indices=False
        )
        theirs = partial_products(cut, grad_out, head, lanes, True, scale)
        parts.append(swap_lanes(theirs, lanes, groups))
        queries = after(queries, cut)
    parts.insert(0, partial_products(queries, grad_out, head, lanes, False, scale))
    share, *sends = cut_by_group(parts, lanes, groups)
    for hop in far_first:
        share = share + hop_groups(sends[hop - 1], hop, lanes, groups).astype(jnp.float32)
    own, first = suffix_sum(share, blocks)
    met = [hop_groups(own, hop, lanes, groups) for hop in far_first]

    saved = gather_groups(saved_state, [(), share], lanes, groups)
    sides = [saved]
    if lanes > 1:
        sides.append(swap_lanes(after(saved, first), lanes, groups))
    grad_q = query_grads(queries, grad_out, sides)

    near = jnp.stack(after([own, *met[::-1]], grad_q))
    grads = key_value_grads(keys, values, near, False, (), lanes)
    if lanes > 1:
        far = swap_lanes(near, lanes, groups)
        grads = key_value_grads(keys, values, far, True, grads, lanes)
    return grad_q, *grads


def solution(mesh):
    tokens = P(("tm", "space"), None)
    return jax.shard_map(
        per_device,
        mesh=mesh,
        in_specs=(tokens, tokens, tokens, tokens, P("tm", None, "space", None)),
        out_specs=(tokens, tokens, tokens),
        check_vma=False,
    )
```

profile of v0, /device:TPU:0, one launch (start us, length us, event | category | flops | bytes accessed | tf_op | source)
XLA Modules:
  0.0 33.2 jit_solution(2238964465847255258)
XLA Ops:
  0.6 1.1 %constant_dynamic-slice_fusion.q_ref = bf16[128,1280]{1,0:T(8,128)(2,1)S(1)} fusion(bf16[128,2560]{1,0:T(8,128)(2,1)} %q_ref.1, s32[]{:T(128)S(6)} %mul.3), kind=kLoop, calls=%fused_computation.10 | loop fusion | bytes 655364 | tf_op jit(solution)/shard_map/dynamic_slice | solution.py:274
  1.7 0.1 copy-done
  1.8 0.3 partial_other.1
  2.1 0.5 %collective-permute-start.1 = (bf16[1280,128]{1,0:T(8,128)(2,1)S(1)}, bf16[1280,128]{1,0:T(8,128)(2,1)S(1)}, u32[]{:S(2)}, u32[]{:S(2)}) collective-permute-start(bf16[1280,128]{1,0:T(8,128)(2,1)S(1)} %partial_other.1), channel_id=1, source_target_pairs={{0,1},{1,0},{2,3},{3,2},{4,5},{5,4},{6,7},{7,6},{8,9},{9,8},{10,11... | collective-permute-start | bytes 983048 | tf_op jit(solution)/shard_map/ppermute | solution.py:50
  2.6 0.1 copy-done.4
  2.7 2.9 %collective-permute-start = (bf16[1,20,16,128]{3,2,1,0:T(8,128)(2,1)S(1)}, bf16[1,20,16,128]{3,2,1,0:T(8,128)(2,1)S(1)}, u32[]{:S(2)}, u32[]{:S(2)}) collective-permute-start(bf16[1,20,16,128]{3,2,1,0:T(8,128)(2,1)S(1)} %copy-done.4), channel_id=1, source_target_pairs={{0,2},{1,3},{2,0},{3,1},{4,6},{5,7},{6,4},{7,5},{8,10},{9,11},{10,... | collective-permute-start | bytes 245768 | tf_op jit(solution)/shard_map/ppermute | solution.py:59
  5.6 0.3 partial_own.1.refs_0_
  5.9 0.1 cut_by_group.1
  6.0 1.8 %collective-permute-start.2 = (bf16[320,128]{1,0:T(8,128)(2,1)S(1)}, bf16[320,128]{1,0:T(8,128)(2,1)S(1)}, u32[]{:S(2)}, u32[]{:S(2)}) collective-permute-start(bf16[320,128]{1,0:T(8,128)(2,1)S(1)} %get-tuple-element.20), channel_id=1, source_target_pairs={{0,6},{1,7},{2,4},{3,5},{4,2},{5,3},{6,0},{7,1},{8,14},{9,15},{10,... | collective-permute-start | bytes 245768 | tf_op jit(solution)/shard_map/ppermute | solution.py:59
  7.8 0.5 %collective-permute-start.3 = (bf16[320,128]{1,0:T(8,128)(2,1)S(1)}, bf16[320,128]{1,0:T(8,128)(2,1)S(1)}, u32[]{:S(2)}, u32[]{:S(2)}) collective-permute-start(bf16[320,128]{1,0:T(8,128)(2,1)S(1)} %get-tuple-element.21), channel_id=1, source_target_pairs={{0,4},{1,5},{2,6},{3,7},{4,0},{5,1},{6,2},{7,3},{8,12},{9,13},{10,... | collective-permute-start | bytes 245768 | tf_op jit(solution)/shard_map/ppermute | solution.py:59
  8.3 1.2 %collective-permute-start.4 = (bf16[320,128]{1,0:T(8,128)(2,1)S(1)}, bf16[320,128]{1,0:T(8,128)(2,1)S(1)}, u32[]{:S(2)}, u32[]{:S(2)}) collective-permute-start(bf16[320,128]{1,0:T(8,128)(2,1)S(1)} %get-tuple-element.22), channel_id=1, source_target_pairs={{0,2},{1,3},{2,0},{3,1},{4,6},{5,7},{6,4},{7,5},{8,10},{9,11},{10,... | collective-permute-start | bytes 245768 | tf_op jit(solution)/shard_map/ppermute | solution.py:59
  9.6 1.9 %collective-permute-done.2 = bf16[320,128]{1,0:T(8,128)(2,1)S(1)} collective-permute-done((bf16[320,128]{1,0:T(8,128)(2,1)S(1)}, bf16[320,128]{1,0:T(8,128)(2,1)S(1)}, u32[]{:S(2)}, u32[]{:S(2)}) %collective-permute-start.2) | collective-permute-done | bytes 81952 | tf_op jit(solution)/shard_map/ppermute | solution.py:59
  11.5 1.6 %collective-permute-done.3 = bf16[320,128]{1,0:T(8,128)(2,1)S(1)} collective-permute-done((bf16[320,128]{1,0:T(8,128)(2,1)S(1)}, bf16[320,128]{1,0:T(8,128)(2,1)S(1)}, u32[]{:S(2)}, u32[]{:S(2)}) %collective-permute-start.3) | collective-permute-done | bytes 81952 | tf_op jit(solution)/shard_map/ppermute | solution.py:59
  13.1 0.1 collective-permute-done.4
  13.2 1.6 %collective-permute-start.6 = (bf16[320,128]{1,0:T(8,128)(2,1)S(1)}, bf16[320,128]{1,0:T(8,128)(2,1)S(1)}, u32[]{:S(2)}, u32[]{:S(2)}) collective-permute-start(bf16[320,128]{1,0:T(8,128)(2,1)S(1)} %get-tuple-element.33), channel_id=1, source_target_pairs={{0,8},{8,0},{16,24},{24,16},{1,9},{9,1},{17,25},{25,17},{2,10},{10... | collective-permute-start | bytes 245768 | tf_op jit(solution)/shard_map/ppermute | solution.py:248
  14.8 1.2 %collective-permute-start.5 = (bf16[2,20,16,128]{3,2,1,0:T(8,128)(2,1)S(1)}, bf16[2,20,16,128]{3,2,1,0:T(8,128)(2,1)S(1)}, u32[]{:S(2)}, u32[]{:S(2)}) collective-permute-start(bf16[2,20,16,128]{3,2,1,0:T(8,128)(2,1)S(1)} %pad_maximum_fusion.1), channel_id=1, source_target_pairs={{0,4},{1,5},{2,6},{3,7},{4,0},{5,1},{6,2},{7,3},{8,12},{9,13},{10,... | collective-permute-start | bytes 491528 | tf_op jit(solution)/shard_map/ppermute | solution.py:59
  16.0 1.7 %collective-permute-done.6 = bf16[320,128]{1,0:T(8,128)(2,1)S(1)} collective-permute-done((bf16[320,128]{1,0:T(8,128)(2,1)S(1)}, bf16[320,128]{1,0:T(8,128)(2,1)S(1)}, u32[]{:S(2)}, u32[]{:S(2)}) %collective-permute-start.6) | collective-permute-done | bytes 81952 | tf_op jit(solution)/shard_map/ppermute | solution.py:248
  17.7 2.7 %collective-permute-start.8 = (bf16[320,128]{1,0:T(8,128)(2,1)S(1)}, bf16[320,128]{1,0:T(8,128)(2,1)S(1)}, u32[]{:S(2)}, u32[]{:S(2)}) collective-permute-start(bf16[320,128]{1,0:T(8,128)(2,1)S(1)} %convert_add_fusion), channel_id=1, source_target_pairs={{0,16},{8,24},{16,0},{24,8},{1,17},{9,25},{17,1},{25,9},{2,18},{10... | collective-permute-start | bytes 245768 | tf_op jit(solution)/shard_map/ppermute | solution.py:248
  20.4 0.1 collective-permute-done.5
  20.5 0.1 collective-permute-start.7
  20.6 2.5 %collective-permute-done.8 = bf16[320,128]{1,0:T(8,128)(2,1)S(1)} collective-permute-done((bf16[320,128]{1,0:T(8,128)(2,1)S(1)}, bf16[320,128]{1,0:T(8,128)(2,1)S(1)}, u32[]{:S(2)}, u32[]{:S(2)}) %collective-permute-start.8) | collective-permute-done | bytes 81952 | tf_op jit(solution)/shard_map/ppermute | solution.py:248
  23.2 1.9 %collective-permute-start.11 = (bf16[320,128]{1,0:T(8,128)(2,1)S(1)}, bf16[320,128]{1,0:T(8,128)(2,1)S(1)}, u32[]{:S(2)}, u32[]{:S(2)}) collective-permute-start(bf16[320,128]{1,0:T(8,128)(2,1)S(1)} %fusion.2), channel_id=1, source_target_pairs={{0,6},{1,7},{2,4},{3,5},{4,2},{5,3},{6,0},{7,1},{8,14},{9,15},{10,... | collective-permute-start | bytes 245768 | tf_op jit(solution)/shard_map/ppermute | solution.py:59
  25.1 0.8 %collective-permute-start.10 = (bf16[320,128]{1,0:T(8,128)(2,1)S(1)}, bf16[320,128]{1,0:T(8,128)(2,1)S(1)}, u32[]{:S(2)}, u32[]{:S(2)}) collective-permute-start(bf16[320,128]{1,0:T(8,128)(2,1)S(1)} %fusion.2), channel_id=1, source_target_pairs={{0,4},{1,5},{2,6},{3,7},{4,0},{5,1},{6,2},{7,3},{8,12},{9,13},{10,... | collective-permute-start | bytes 245768 | tf_op jit(solution)/shard_map/ppermute | solution.py:59
  25.9 0.9 %collective-permute-start.9 = (bf16[320,128]{1,0:T(8,128)(2,1)S(1)}, bf16[320,128]{1,0:T(8,128)(2,1)S(1)}, u32[]{:S(2)}, u32[]{:S(2)}) collective-permute-start(bf16[320,128]{1,0:T(8,128)(2,1)S(1)} %fusion.2), channel_id=1, source_target_pairs={{0,2},{1,3},{2,0},{3,1},{4,6},{5,7},{6,4},{7,5},{8,10},{9,11},{10,... | collective-permute-start | bytes 245768 | tf_op jit(solution)/shard_map/ppermute | solution.py:59
  26.7 1.6 %query_grads.1 = bf16[128,2560]{1,0:T(8,128)(2,1)} custom-call(bf16[128,2560]{1,0:T(8,128)(2,1)S(1)} %copy-done.1, bf16[128,2560]{1,0:T(8,128)(2,1)S(1)} %copy-done, bf16[4,20,16,128]{3,2,1,0:T(8,128)(2,1)S(1)} %constant_dynamic-update-slice_fusion.rest_0_, bf16[4,20,16,128]{3,2,1,0:T(8,128)(2,1)S(1)} %collective-permute-done.7.rest_1_), custom_call_target="tpu_custom_call" | custom-call | flops 83886080 | bytes 2621440 | tf_op jit(solution)/shard_map/query_grads/pallas_call | solution.py:167
  28.3 0.3 collective-permute-done.11
  28.6 0.9 %collective-permute-done.10 = bf16[320,128]{1,0:T(8,128)(2,1)S(1)} collective-permute-done((bf16[320,128]{1,0:T(8,128)(2,1)S(1)}, bf16[320,128]{1,0:T(8,128)(2,1)S(1)}, u32[]{:S(2)}, u32[]{:S(2)}) %collective-permute-start.10) | collective-permute-done | bytes 81952 | tf_op jit(solution)/shard_map/ppermute | solution.py:59
  29.5 0.8 %collective-permute-done.9 = bf16[320,128]{1,0:T(8,128)(2,1)S(1)} collective-permute-done((bf16[320,128]{1,0:T(8,128)(2,1)S(1)}, bf16[320,128]{1,0:T(8,128)(2,1)S(1)}, u32[]{:S(2)}, u32[]{:S(2)}) %collective-permute-start.9) | collective-permute-done | bytes 81952 | tf_op jit(solution)/shard_map/ppermute | solution.py:59
  30.4 0.1 collective-permute-start.12
  30.5 1.2 %key_value_own.1 = (bf16[128,2560]{1,0:T(8,128)(2,1)}, bf16[128,2560]{1,0:T(8,128)(2,1)}) custom-call(bf16[128,2560]{1,0:T(8,128)(2,1)S(1)} %copy-done.2, bf16[128,2560]{1,0:T(8,128)(2,1)S(1)} %copy-done.3, bf16[4,320,128]{2,1,0:T(8,128)(2,1)S(1)} %pad_maximum_fusion.state_ref), custom_call_target="tpu_custom_call" | custom-call | flops 83886080 | bytes 655360 | tf_op jit(solution)/shard_map/key_value_own/pallas_call | solution.py:220
  31.6 0.4 %collective-permute-done.12.state_ref = bf16[4,320,128]{2,1,0:T(8,128)(2,1)S(1)} collective-permute-done((bf16[4,320,128]{2,1,0:T(8,128)(2,1)S(1)}, bf16[4,320,128]{2,1,0:T(8,128)(2,1)S(1)}, u32[]{:S(2)}, u32[]{:S(2)}) %collective-permute-start.12) | collective-permute-done | bytes 327712 | tf_op jit(solution)/shard_map/ppermute | solution.py:50
  32.0 1.2 %key_value_other.1 = (bf16[128,2560]{1,0:T(8,128)(2,1)}, bf16[128,2560]{1,0:T(8,128)(2,1)}) custom-call(bf16[128,2560]{1,0:T(8,128)(2,1)S(1)} %copy-done.2, bf16[128,2560]{1,0:T(8,128)(2,1)S(1)} %copy-done.3, bf16[4,320,128]{2,1,0:T(8,128)(2,1)S(1)} %collective-permute-done.12.state_ref, ...), custom_call_target="tpu_custom_call", output_to_operand_aliasing={{0}: (3, {}), {1}: (4, {})} | custom-call | flops 83886080 | bytes 655360 | tf_op jit(solution)/shard_map/key_value_other/pallas_call | solution.py:220
  (18 shorter events, 0.2 us)
Async XLA Ops:
  0.6 1.2 %copy-start = (bf16[128,2560]{1,0:T(8,128)(2,1)S(1)}, bf16[128,2560]{1,0:T(8,128)(2,1)}, u32[]{:S(2)}) copy-start(bf16[128,2560]{1,0:T(8,128)(2,1)} %o_ref.5) | copy-start | bytes 1966084
  1.8 0.9 %copy-start.4 = (bf16[1,20,16,128]{3,2,1,0:T(8,128)(2,1)S(1)}, bf16[1,20,16,128]{3,2,1,0:T(8,128)(2,1)}, u32[]{:S(2)}) copy-start(bf16[1,20,16,128]{3,2,1,0:T(8,128)(2,1)} %param.9) | copy-start | bytes 245764
  1.8 3.8 %copy-start.1 = (bf16[128,2560]{1,0:T(8,128)(2,1)S(1)}, bf16[128,2560]{1,0:T(8,128)(2,1)}, u32[]{:S(2)}) copy-start(bf16[128,2560]{1,0:T(8,128)(2,1)} %q_ref.1) | copy-start | bytes 1966084
  2.1 3.8 %collective-permute-start.1 = (bf16[1280,128]{1,0:T(8,128)(2,1)S(1)}, bf16[1280,128]{1,0:T(8,128)(2,1)S(1)}, u32[]{:S(2)}, u32[]{:S(2)}) collective-permute-start(bf16[1280,128]{1,0:T(8,128)(2,1)S(1)} %partial_other.1), channel_id=1, source_target_pairs={{0,1},{1,0},{2,3},{3,2},{4,5},{5,4},{6,7},{7,6},{8,9},{9,8},{10,11... | collective-permute-start | bytes 983048 | tf_op jit(solution)/shard_map/ppermute | solution.py:50
  2.7 6.9 %collective-permute-start = (bf16[1,20,16,128]{3,2,1,0:T(8,128)(2,1)S(1)}, bf16[1,20,16,128]{3,2,1,0:T(8,128)(2,1)S(1)}, u32[]{:S(2)}, u32[]{:S(2)}) collective-permute-start(bf16[1,20,16,128]{3,2,1,0:T(8,128)(2,1)S(1)} %copy-done.4), channel_id=1, source_target_pairs={{0,2},{1,3},{2,0},{3,1},{4,6},{5,7},{6,4},{7,5},{8,10},{9,11},{10,... | collective-permute-start | bytes 245768 | tf_op jit(solution)/shard_map/ppermute | solution.py:59
  6.0 5.5 %collective-permute-start.2 = (bf16[320,128]{1,0:T(8,128)(2,1)S(1)}, bf16[320,128]{1,0:T(8,128)(2,1)S(1)}, u32[]{:S(2)}, u32[]{:S(2)}) collective-permute-start(bf16[320,128]{1,0:T(8,128)(2,1)S(1)} %get-tuple-element.20), channel_id=1, source_target_pairs={{0,6},{1,7},{2,4},{3,5},{4,2},{5,3},{6,0},{7,1},{8,14},{9,15},{10,... | collective-permute-start | bytes 245768 | tf_op jit(solution)/shard_map/ppermute | solution.py:59
  7.8 5.2 %collective-permute-start.3 = (bf16[320,128]{1,0:T(8,128)(2,1)S(1)}, bf16[320,128]{1,0:T(8,128)(2,1)S(1)}, u32[]{:S(2)}, u32[]{:S(2)}) collective-permute-start(bf16[320,128]{1,0:T(8,128)(2,1)S(1)} %get-tuple-element.21), channel_id=1, source_target_pairs={{0,4},{1,5},{2,6},{3,7},{4,0},{5,1},{6,2},{7,3},{8,12},{9,13},{10,... | collective-permute-start | bytes 245768 | tf_op jit(solution)/shard_map/ppermute | solution.py:59
  8.3 4.8 %collective-permute-start.4 = (bf16[320,128]{1,0:T(8,128)(2,1)S(1)}, bf16[320,128]{1,0:T(8,128)(2,1)S(1)}, u32[]{:S(2)}, u32[]{:S(2)}) collective-permute-start(bf16[320,128]{1,0:T(8,128)(2,1)S(1)} %get-tuple-element.22), channel_id=1, source_target_pairs={{0,2},{1,3},{2,0},{3,1},{4,6},{5,7},{6,4},{7,5},{8,10},{9,11},{10,... | collective-permute-start | bytes 245768 | tf_op jit(solution)/shard_map/ppermute | solution.py:59
  13.2 4.5 %collective-permute-start.6 = (bf16[320,128]{1,0:T(8,128)(2,1)S(1)}, bf16[320,128]{1,0:T(8,128)(2,1)S(1)}, u32[]{:S(2)}, u32[]{:S(2)}) collective-permute-start(bf16[320,128]{1,0:T(8,128)(2,1)S(1)} %get-tuple-element.33), channel_id=1, source_target_pairs={{0,8},{8,0},{16,24},{24,16},{1,9},{9,1},{17,25},{25,17},{2,10},{10... | collective-permute-start | bytes 245768 | tf_op jit(solution)/shard_map/ppermute | solution.py:248
  14.8 5.7 %collective-permute-start.5 = (bf16[2,20,16,128]{3,2,1,0:T(8,128)(2,1)S(1)}, bf16[2,20,16,128]{3,2,1,0:T(8,128)(2,1)S(1)}, u32[]{:S(2)}, u32[]{:S(2)}) collective-permute-start(bf16[2,20,16,128]{3,2,1,0:T(8,128)(2,1)S(1)} %pad_maximum_fusion.1), channel_id=1, source_target_pairs={{0,4},{1,5},{2,6},{3,7},{4,0},{5,1},{6,2},{7,3},{8,12},{9,13},{10,... | collective-permute-start | bytes 491528 | tf_op jit(solution)/shard_map/ppermute | solution.py:59
  17.7 5.4 %collective-permute-start.8 = (bf16[320,128]{1,0:T(8,128)(2,1)S(1)}, bf16[320,128]{1,0:T(8,128)(2,1)S(1)}, u32[]{:S(2)}, u32[]{:S(2)}) collective-permute-start(bf16[320,128]{1,0:T(8,128)(2,1)S(1)} %convert_add_fusion), channel_id=1, source_target_pairs={{0,16},{8,24},{16,0},{24,8},{1,17},{9,25},{17,1},{25,9},{2,18},{10... | collective-permute-start | bytes 245768 | tf_op jit(solution)/shard_map/ppermute | solution.py:248
  20.5 6.2 %collective-permute-start.7 = (bf16[4,20,16,128]{3,2,1,0:T(8,128)(2,1)S(1)}, bf16[4,20,16,128]{3,2,1,0:T(8,128)(2,1)S(1)}, u32[]{:S(2)}, u32[]{:S(2)}) collective-permute-start(bf16[4,20,16,128]{3,2,1,0:T(8,128)(2,1)S(1)} %constant_dynamic-update-slice_fusion.rest_0_), channel_id=1, source_target_pairs={{0,1},{1,0},{2,3},{3,2},{4,5},{5,4},{6,7},{7,6},{8,9},{9,8},{10,11... | collective-permute-start | bytes 983048 | tf_op jit(solution)/shard_map/ppermute | solution.py:50
  23.2 5.4 %collective-permute-start.11 = (bf16[320,128]{1,0:T(8,128)(2,1)S(1)}, bf16[320,128]{1,0:T(8,128)(2,1)S(1)}, u32[]{:S(2)}, u32[]{:S(2)}) collective-permute-start(bf16[320,128]{1,0:T(8,128)(2,1)S(1)} %fusion.2), channel_id=1, source_target_pairs={{0,6},{1,7},{2,4},{3,5},{4,2},{5,3},{6,0},{7,1},{8,14},{9,15},{10,... | collective-permute-start | bytes 245768 | tf_op jit(solution)/shard_map/ppermute | solution.py:59
  25.1 4.4 %collective-permute-start.10 = (bf16[320,128]{1,0:T(8,128)(2,1)S(1)}, bf16[320,128]{1,0:T(8,128)(2,1)S(1)}, u32[]{:S(2)}, u32[]{:S(2)}) collective-permute-start(bf16[320,128]{1,0:T(8,128)(2,1)S(1)} %fusion.2), channel_id=1, source_target_pairs={{0,4},{1,5},{2,6},{3,7},{4,0},{5,1},{6,2},{7,3},{8,12},{9,13},{10,... | collective-permute-start | bytes 245768 | tf_op jit(solution)/shard_map/ppermute | solution.py:59
  25.9 4.4 %collective-permute-start.9 = (bf16[320,128]{1,0:T(8,128)(2,1)S(1)}, bf16[320,128]{1,0:T(8,128)(2,1)S(1)}, u32[]{:S(2)}, u32[]{:S(2)}) collective-permute-start(bf16[320,128]{1,0:T(8,128)(2,1)S(1)} %fusion.2), channel_id=1, source_target_pairs={{0,2},{1,3},{2,0},{3,1},{4,6},{5,7},{6,4},{7,5},{8,10},{9,11},{10,... | collective-permute-start | bytes 245768 | tf_op jit(solution)/shard_map/ppermute | solution.py:59
  26.7 3.7 %copy-start.3 = (bf16[128,2560]{1,0:T(8,128)(2,1)S(1)}, bf16[128,2560]{1,0:T(8,128)(2,1)}, u32[]{:S(2)}) copy-start(bf16[128,2560]{1,0:T(8,128)(2,1)} %v_ref.3) | copy-start | bytes 1966084
  28.3 2.2 %copy-start.2 = (bf16[128,2560]{1,0:T(8,128)(2,1)S(1)}, bf16[128,2560]{1,0:T(8,128)(2,1)}, u32[]{:S(2)}) copy-start(bf16[128,2560]{1,0:T(8,128)(2,1)} %k_ref.3) | copy-start | bytes 1966084
  30.4 1.7 %collective-permute-start.12 = (bf16[4,320,128]{2,1,0:T(8,128)(2,1)S(1)}, bf16[4,320,128]{2,1,0:T(8,128)(2,1)S(1)}, u32[]{:S(2)}, u32[]{:S(2)}) collective-permute-start(bf16[4,320,128]{2,1,0:T(8,128)(2,1)S(1)} %pad_maximum_fusion.state_ref), channel_id=1, source_target_pairs={{0,1},{1,0},{2,3},{3,2},{4,5},{5,4},{6,7},{7,6},{8,9},{9,8},{10,11... | collective-permute-start | bytes 983048 | tf_op jit(solution)/shard_map/ppermute | solution.py:50
where the time goes:
time: 33.4 us; the launch traced here: 33.2 us
  starting transfers between devices  16.2 us (49%)
  waiting for transfers between devices  10.3 us (31%)
  Pallas kernels  4.57 us (14%)
  local copies, waits for them, and re-layouts  1.29 us (4%)
  between operations  0.78 us (2%)
    ppermute x8, starting transfers between devices, hop_groups(): return lax.ppermute(value, 'space', pairs)  11.2 us
    ppermute x8, waiting for transfers between devices, hop_groups(): return lax.ppermute(value, 'space', pairs)  5.69 us
    ppermute x2, starting transfers between devices, suffix_sum(): lax.ppermute(total.astype(jnp.bfloat16), 'tm', pairs).astype(jnp.float32)  4.3 us
    ppermute x2, waiting for transfers between devices, suffix_sum(): lax.ppermute(total.astype(jnp.bfloat16), 'tm', pairs).astype(jnp.float32)  4.18 us
    pallas_call x2, Pallas kernels, key_value_grads(): pl.pallas_call(functools.partial(key_value_kernel, lanes, other, steps),...  2.37 us
    pallas_call x1, Pallas kernels, query_grads(): pl.pallas_call(functools.partial(query_kernel, lanes), out_shape=jax.Shap...  1.56 us
    dynamic_slice x1, local copies, waits for them, and re-layouts, per_device(): lax.dynamic_slice(queries, starts, (queries.shape[0], span), allow_negati...  1.06 us
  transfers between devices with their start and end apart: 13, of which 10 were waited for; matrix products, arithmetic and copies ran while one was open for 0% of the time, Pallas kernels for 9%

commit v1 on v0

--- a/solution.py
+++ b/solution.py
@@ -284,7 +284,7 @@
     own, first = suffix_sum(share, blocks)
     met = [hop_groups(own, hop, lanes, groups) for hop in far_first]
 
-    saved = gather_groups(saved_state, [(), share], lanes, groups)
+    saved = gather_groups(saved_state, [parts[0], share], lanes, groups)
     sides = [saved]
     if lanes > 1:
         sides.append(swap_lanes(after(saved, first), lanes, groups))

time: 33.4 us -> 33.4 us (level)
    ppermute x8, waiting for transfers between devices: 5.69 us -> 5.26 us  [hop_groups(): return lax.ppermute(value, 'space', pairs)]
    ppermute x2, waiting for transfers between devices: 4.18 us -> 4.51 us  [suffix_sum(): lax.ppermute(total.astype(jnp.bfloat16), 'tm', pairs).astype(jnp.float32)]
  transfers between devices with their start and end apart: 13 -> 13, of which waited for: 10 -> 8; matrix products, arithmetic and copies ran while one was open for 0% -> 0% of each run, Pallas kernels for 9% -> 9%
where the time goes in v1:
time: 33.4 us; the launch traced here: 33.2 us
  starting transfers between devices  16 us (48%)
  waiting for transfers between devices  10.2 us (31%)
  Pallas kernels  4.56 us (14%)
  local copies, waits for them, and re-layouts  1.49 us (4%)
  between operations  0.78 us (2%)
    ppermute x8, starting transfers between devices, hop_groups(): return lax.ppermute(value, 'space', pairs)  11.1 us
    ppermute x8, waiting for transfers between devices, hop_groups(): return lax.ppermute(value, 'space', pairs)  5.26 us
    ppermute x2, waiting for transfers between devices, suffix_sum(): lax.ppermute(total.astype(jnp.bfloat16), 'tm', pairs).astype(jnp.float32)  4.51 us
    ppermute x2, starting transfers between devices, suffix_sum(): lax.ppermute(total.astype(jnp.bfloat16), 'tm', pairs).astype(jnp.float32)  4.29 us
    pallas_call x2, Pallas kernels, key_value_grads(): pl.pallas_call(functools.partial(key_value_kernel, lanes, other, steps),...  2.38 us
    pallas_call x1, Pallas kernels, query_grads(): pl.pallas_call(functools.partial(query_kernel, lanes), out_shape=jax.Shap...  1.56 us
    dynamic_slice x1, local copies, waits for them, and re-layouts, per_device(): lax.dynamic_slice(queries, starts, (queries.shape[0], span), allow_negati...  1.06 us
  transfers between devices with their start and end apart: 13, of which 8 were waited for; matrix products, arithmetic and copies ran while one was open for 0% of the time, Pallas kernels for 9%

profile of v1, /device:TPU:0, one launch (start us, length us, event | category | flops | bytes accessed | tf_op | source)
XLA Modules:
  0.0 33.2 jit_solution(4566950938300501467)
XLA Ops:
  0.6 1.1 %constant_dynamic-slice_fusion.q_ref = bf16[128,1280]{1,0:T(8,128)(2,1)S(1)} fusion(bf16[128,2560]{1,0:T(8,128)(2,1)} %q_ref.1, s32[]{:T(128)S(6)} %mul.3), kind=kLoop, calls=%fused_computation.10 | loop fusion | bytes 655364 | tf_op jit(solution)/shard_map/dynamic_slice | solution.py:274
  1.7 0.1 copy-done
  1.8 0.3 partial_other.1
  2.1 0.0 copy-start.4
  2.1 0.5 %collective-permute-start.1 = (bf16[1280,128]{1,0:T(8,128)(2,1)S(1)}, bf16[1280,128]{1,0:T(8,128)(2,1)S(1)}, u32[]{:S(2)}, u32[]{:S(2)}) collective-permute-start(bf16[1280,128]{1,0:T(8,128)(2,1)S(1)} %partial_other.1), channel_id=1, source_target_pairs={{0,1},{1,0},{2,3},{3,2},{4,5},{5,4},{6,7},{7,6},{8,9},{9,8},{10,11... | collective-permute-start | bytes 983048 | tf_op jit(solution)/shard_map/ppermute | solution.py:50
  2.6 0.3 copy-done.1
  2.9 0.3 partial_own.1.refs_0_
  3.2 3.0 %collective-permute-start = (bf16[1,20,16,128]{3,2,1,0:T(8,128)(2,1)S(1)}, bf16[1,20,16,128]{3,2,1,0:T(8,128)(2,1)S(1)}, u32[]{:S(2)}, u32[]{:S(2)}) collective-permute-start(bf16[1,20,16,128]{3,2,1,0:T(8,128)(2,1)S(1)} %copy-done.4), channel_id=1, source_target_pairs={{0,2},{1,3},{2,0},{3,1},{4,6},{5,7},{6,4},{7,5},{8,10},{9,11},{10,... | collective-permute-start | bytes 245768 | tf_op jit(solution)/shard_map/ppermute | solution.py:59
  6.2 0.1 cut_by_group.1
  6.3 1.6 %collective-permute-start.2 = (bf16[320,128]{1,0:T(8,128)(2,1)S(1)}, bf16[320,128]{1,0:T(8,128)(2,1)S(1)}, u32[]{:S(2)}, u32[]{:S(2)}) collective-permute-start(bf16[320,128]{1,0:T(8,128)(2,1)S(1)} %get-tuple-element.22), channel_id=1, source_target_pairs={{0,6},{1,7},{2,4},{3,5},{4,2},{5,3},{6,0},{7,1},{8,14},{9,15},{10,... | collective-permute-start | bytes 245768 | tf_op jit(solution)/shard_map/ppermute | solution.py:59
  7.8 0.5 %collective-permute-start.3 = (bf16[320,128]{1,0:T(8,128)(2,1)S(1)}, bf16[320,128]{1,0:T(8,128)(2,1)S(1)}, u32[]{:S(2)}, u32[]{:S(2)}) collective-permute-start(bf16[320,128]{1,0:T(8,128)(2,1)S(1)} %get-tuple-element.23), channel_id=1, source_target_pairs={{0,4},{1,5},{2,6},{3,7},{4,0},{5,1},{6,2},{7,3},{8,12},{9,13},{10,... | collective-permute-start | bytes 245768 | tf_op jit(solution)/shard_map/ppermute | solution.py:59
  8.3 1.5 %collective-permute-start.4 = (bf16[320,128]{1,0:T(8,128)(2,1)S(1)}, bf16[320,128]{1,0:T(8,128)(2,1)S(1)}, u32[]{:S(2)}, u32[]{:S(2)}) collective-permute-start(bf16[320,128]{1,0:T(8,128)(2,1)S(1)} %get-tuple-element.24), channel_id=1, source_target_pairs={{0,2},{1,3},{2,0},{3,1},{4,6},{5,7},{6,4},{7,5},{8,10},{9,11},{10,... | collective-permute-start | bytes 245768 | tf_op jit(solution)/shard_map/ppermute | solution.py:59
  9.8 2.3 %collective-permute-done.2 = bf16[320,128]{1,0:T(8,128)(2,1)S(1)} collective-permute-done((bf16[320,128]{1,0:T(8,128)(2,1)S(1)}, bf16[320,128]{1,0:T(8,128)(2,1)S(1)}, u32[]{:S(2)}, u32[]{:S(2)}) %collective-permute-start.2) | collective-permute-done | bytes 81952 | tf_op jit(solution)/shard_map/ppermute | solution.py:59
  12.2 1.2 %collective-permute-done.3 = bf16[320,128]{1,0:T(8,128)(2,1)S(1)} collective-permute-done((bf16[320,128]{1,0:T(8,128)(2,1)S(1)}, bf16[320,128]{1,0:T(8,128)(2,1)S(1)}, u32[]{:S(2)}, u32[]{:S(2)}) %collective-permute-start.3) | collective-permute-done | bytes 81952 | tf_op jit(solution)/shard_map/ppermute | solution.py:59
  13.4 1.6 %collective-permute-start.6 = (bf16[320,128]{1,0:T(8,128)(2,1)S(1)}, bf16[320,128]{1,0:T(8,128)(2,1)S(1)}, u32[]{:S(2)}, u32[]{:S(2)}) collective-permute-start(bf16[320,128]{1,0:T(8,128)(2,1)S(1)} %get-tuple-element.35), channel_id=1, source_target_pairs={{0,8},{8,0},{16,24},{24,16},{1,9},{9,1},{17,25},{25,17},{2,10},{10... | collective-permute-start | bytes 245768 | tf_op jit(solution)/shard_map/ppermute | solution.py:248
  15.0 1.0 %collective-permute-start.5 = (bf16[2,20,16,128]{3,2,1,0:T(8,128)(2,1)S(1)}, bf16[2,20,16,128]{3,2,1,0:T(8,128)(2,1)S(1)}, u32[]{:S(2)}, u32[]{:S(2)}) collective-permute-start(bf16[2,20,16,128]{3,2,1,0:T(8,128)(2,1)S(1)} %pad_maximum_fusion.1), channel_id=1, source_target_pairs={{0,4},{1,5},{2,6},{3,7},{4,0},{5,1},{6,2},{7,3},{8,12},{9,13},{10,... | collective-permute-start | bytes 491528 | tf_op jit(solution)/shard_map/ppermute | solution.py:59
  16.0 1.9 %collective-permute-done.6 = bf16[320,128]{1,0:T(8,128)(2,1)S(1)} collective-permute-done((bf16[320,128]{1,0:T(8,128)(2,1)S(1)}, bf16[320,128]{1,0:T(8,128)(2,1)S(1)}, u32[]{:S(2)}, u32[]{:S(2)}) %collective-permute-start.6) | collective-permute-done | bytes 81952 | tf_op jit(solution)/shard_map/ppermute | solution.py:248
  17.9 2.7 %collective-permute-start.8 = (bf16[320,128]{1,0:T(8,128)(2,1)S(1)}, bf16[320,128]{1,0:T(8,128)(2,1)S(1)}, u32[]{:S(2)}, u32[]{:S(2)}) collective-permute-start(bf16[320,128]{1,0:T(8,128)(2,1)S(1)} %convert_add_fusion), channel_id=1, source_target_pairs={{0,16},{8,24},{16,0},{24,8},{1,17},{9,25},{17,1},{25,9},{2,18},{10... | collective-permute-start | bytes 245768 | tf_op jit(solution)/shard_map/ppermute | solution.py:248
  20.6 0.0 collective-permute-done.5
  20.6 0.1 collective-permute-start.7
  20.7 2.6 %collective-permute-done.8 = bf16[320,128]{1,0:T(8,128)(2,1)S(1)} collective-permute-done((bf16[320,128]{1,0:T(8,128)(2,1)S(1)}, bf16[320,128]{1,0:T(8,128)(2,1)S(1)}, u32[]{:S(2)}, u32[]{:S(2)}) %collective-permute-start.8) | collective-permute-done | bytes 81952 | tf_op jit(solution)/shard_map/ppermute | solution.py:248
  23.4 1.9 %collective-permute-start.11 = (bf16[320,128]{1,0:T(8,128)(2,1)S(1)}, bf16[320,128]{1,0:T(8,128)(2,1)S(1)}, u32[]{:S(2)}, u32[]{:S(2)}) collective-permute-start(bf16[320,128]{1,0:T(8,128)(2,1)S(1)} %fusion.2), channel_id=1, source_target_pairs={{0,6},{1,7},{2,4},{3,5},{4,2},{5,3},{6,0},{7,1},{8,14},{9,15},{10,... | collective-permute-start | bytes 245768 | tf_op jit(solution)/shard_map/ppermute | solution.py:59
  25.3 0.5 %collective-permute-start.10 = (bf16[320,128]{1,0:T(8,128)(2,1)S(1)}, bf16[320,128]{1,0:T(8,128)(2,1)S(1)}, u32[]{:S(2)}, u32[]{:S(2)}) collective-permute-start(bf16[320,128]{1,0:T(8,128)(2,1)S(1)} %fusion.2), channel_id=1, source_target_pairs={{0,4},{1,5},{2,6},{3,7},{4,0},{5,1},{6,2},{7,3},{8,12},{9,13},{10,... | collective-permute-start | bytes 245768 | tf_op jit(solution)/shard_map/ppermute | solution.py:59
  25.8 1.1 %collective-permute-start.9 = (bf16[320,128]{1,0:T(8,128)(2,1)S(1)}, bf16[320,128]{1,0:T(8,128)(2,1)S(1)}, u32[]{:S(2)}, u32[]{:S(2)}) collective-permute-start(bf16[320,128]{1,0:T(8,128)(2,1)S(1)} %fusion.2), channel_id=1, source_target_pairs={{0,2},{1,3},{2,0},{3,1},{4,6},{5,7},{6,4},{7,5},{8,10},{9,11},{10,... | collective-permute-start | bytes 245768 | tf_op jit(solution)/shard_map/ppermute | solution.py:59
  26.9 1.6 %query_grads.1 = bf16[128,2560]{1,0:T(8,128)(2,1)} custom-call(bf16[128,2560]{1,0:T(8,128)(2,1)S(1)} %copy-done.1, bf16[128,2560]{1,0:T(8,128)(2,1)S(1)} %copy-done, bf16[4,20,16,128]{3,2,1,0:T(8,128)(2,1)S(1)} %constant_dynamic-update-slice_fusion.rest_0_, bf16[4,20,16,128]{3,2,1,0:T(8,128)(2,1)S(1)} %collective-permute-done.7.rest_1_), custom_call_target="tpu_custom_call" | custom-call | flops 83886080 | bytes 2621440 | tf_op jit(solution)/shard_map/query_grads/pallas_call | solution.py:167
  28.5 0.3 collective-permute-done.11
  28.8 1.0 %collective-permute-done.10 = bf16[320,128]{1,0:T(8,128)(2,1)S(1)} collective-permute-done((bf16[320,128]{1,0:T(8,128)(2,1)S(1)}, bf16[320,128]{1,0:T(8,128)(2,1)S(1)}, u32[]{:S(2)}, u32[]{:S(2)}) %collective-permute-start.10) | collective-permute-done | bytes 81952 | tf_op jit(solution)/shard_map/ppermute | solution.py:59
  29.8 0.5 %collective-permute-done.9 = bf16[320,128]{1,0:T(8,128)(2,1)S(1)} collective-permute-done((bf16[320,128]{1,0:T(8,128)(2,1)S(1)}, bf16[320,128]{1,0:T(8,128)(2,1)S(1)}, u32[]{:S(2)}, u32[]{:S(2)}) %collective-permute-start.9) | collective-permute-done | bytes 81952 | tf_op jit(solution)/shard_map/ppermute | solution.py:59
  30.3 0.1 collective-permute-start.12
  30.4 1.2 %key_value_own.1 = (bf16[128,2560]{1,0:T(8,128)(2,1)}, bf16[128,2560]{1,0:T(8,128)(2,1)}) custom-call(bf16[128,2560]{1,0:T(8,128)(2,1)S(1)} %copy-done.2, bf16[128,2560]{1,0:T(8,128)(2,1)S(1)} %copy-done.3, bf16[4,320,128]{2,1,0:T(8,128)(2,1)S(1)} %pad_maximum_fusion.state_ref), custom_call_target="tpu_custom_call" | custom-call | flops 83886080 | bytes 655360 | tf_op jit(solution)/shard_map/key_value_own/pallas_call | solution.py:220
  31.6 0.4 %collective-permute-done.12.state_ref = bf16[4,320,128]{2,1,0:T(8,128)(2,1)S(1)} collective-permute-done((bf16[4,320,128]{2,1,0:T(8,128)(2,1)S(1)}, bf16[4,320,128]{2,1,0:T(8,128)(2,1)S(1)}, u32[]{:S(2)}, u32[]{:S(2)}) %collective-permute-start.12) | collective-permute-done | bytes 327712 | tf_op jit(solution)/shard_map/ppermute | solution.py:50
  32.0 1.2 %key_value_other.1 = (bf16[128,2560]{1,0:T(8,128)(2,1)}, bf16[128,2560]{1,0:T(8,128)(2,1)}) custom-call(bf16[128,2560]{1,0:T(8,128)(2,1)S(1)} %copy-done.2, bf16[128,2560]{1,0:T(8,128)(2,1)S(1)} %copy-done.3, bf16[4,320,128]{2,1,0:T(8,128)(2,1)S(1)} %collective-permute-done.12.state_ref, ...), custom_call_target="tpu_custom_call", output_to_operand_aliasing={{0}: (3, {}), {1}: (4, {})} | custom-call | flops 83886080 | bytes 655360 | tf_op jit(solution)/shard_map/key_value_other/pallas_call | solution.py:220
  (18 shorter events, 0.2 us)
Async XLA Ops:
  0.6 1.2 %copy-start = (bf16[128,2560]{1,0:T(8,128)(2,1)S(1)}, bf16[128,2560]{1,0:T(8,128)(2,1)}, u32[]{:S(2)}) copy-start(bf16[128,2560]{1,0:T(8,128)(2,1)} %o_ref.5) | copy-start | bytes 1966084
  1.8 1.1 %copy-start.1 = (bf16[128,2560]{1,0:T(8,128)(2,1)S(1)}, bf16[128,2560]{1,0:T(8,128)(2,1)}, u32[]{:S(2)}) copy-start(bf16[128,2560]{1,0:T(8,128)(2,1)} %q_ref.1) | copy-start | bytes 1966084
  2.1 1.1 %copy-start.4 = (bf16[1,20,16,128]{3,2,1,0:T(8,128)(2,1)S(1)}, bf16[1,20,16,128]{3,2,1,0:T(8,128)(2,1)}, u32[]{:S(2)}) copy-start(bf16[1,20,16,128]{3,2,1,0:T(8,128)(2,1)} %param.9) | copy-start | bytes 245764
  2.1 4.1 %collective-permute-start.1 = (bf16[1280,128]{1,0:T(8,128)(2,1)S(1)}, bf16[1280,128]{1,0:T(8,128)(2,1)S(1)}, u32[]{:S(2)}, u32[]{:S(2)}) collective-permute-start(bf16[1280,128]{1,0:T(8,128)(2,1)S(1)} %partial_other.1), channel_id=1, source_target_pairs={{0,1},{1,0},{2,3},{3,2},{4,5},{5,4},{6,7},{7,6},{8,9},{9,8},{10,11... | collective-permute-start | bytes 983048 | tf_op jit(solution)/shard_map/ppermute | solution.py:50
  3.2 6.6 %collective-permute-start = (bf16[1,20,16,128]{3,2,1,0:T(8,128)(2,1)S(1)}, bf16[1,20,16,128]{3,2,1,0:T(8,128)(2,1)S(1)}, u32[]{:S(2)}, u32[]{:S(2)}) collective-permute-start(bf16[1,20,16,128]{3,2,1,0:T(8,128)(2,1)S(1)} %copy-done.4), channel_id=1, source_target_pairs={{0,2},{1,3},{2,0},{3,1},{4,6},{5,7},{6,4},{7,5},{8,10},{9,11},{10,... | collective-permute-start | bytes 245768 | tf_op jit(solution)/shard_map/ppermute | solution.py:59
  6.3 5.9 %collective-permute-start.2 = (bf16[320,128]{1,0:T(8,128)(2,1)S(1)}, bf16[320,128]{1,0:T(8,128)(2,1)S(1)}, u32[]{:S(2)}, u32[]{:S(2)}) collective-permute-start(bf16[320,128]{1,0:T(8,128)(2,1)S(1)} %get-tuple-element.22), channel_id=1, source_target_pairs={{0,6},{1,7},{2,4},{3,5},{4,2},{5,3},{6,0},{7,1},{8,14},{9,15},{10,... | collective-permute-start | bytes 245768 | tf_op jit(solution)/shard_map/ppermute | solution.py:59
  7.8 5.5 %collective-permute-start.3 = (bf16[320,128]{1,0:T(8,128)(2,1)S(1)}, bf16[320,128]{1,0:T(8,128)(2,1)S(1)}, u32[]{:S(2)}, u32[]{:S(2)}) collective-permute-start(bf16[320,128]{1,0:T(8,128)(2,1)S(1)} %get-tuple-element.23), channel_id=1, source_target_pairs={{0,4},{1,5},{2,6},{3,7},{4,0},{5,1},{6,2},{7,3},{8,12},{9,13},{10,... | collective-permute-start | bytes 245768 | tf_op jit(solution)/shard_map/ppermute | solution.py:59
  8.3 5.0 %collective-permute-start.4 = (bf16[320,128]{1,0:T(8,128)(2,1)S(1)}, bf16[320,128]{1,0:T(8,128)(2,1)S(1)}, u32[]{:S(2)}, u32[]{:S(2)}) collective-permute-start(bf16[320,128]{1,0:T(8,128)(2,1)S(1)} %get-tuple-element.24), channel_id=1, source_target_pairs={{0,2},{1,3},{2,0},{3,1},{4,6},{5,7},{6,4},{7,5},{8,10},{9,11},{10,... | collective-permute-start | bytes 245768 | tf_op jit(solution)/shard_map/ppermute | solution.py:59
  13.4 4.5 %collective-permute-start.6 = (bf16[320,128]{1,0:T(8,128)(2,1)S(1)}, bf16[320,128]{1,0:T(8,128)(2,1)S(1)}, u32[]{:S(2)}, u32[]{:S(2)}) collective-permute-start(bf16[320,128]{1,0:T(8,128)(2,1)S(1)} %get-tuple-element.35), channel_id=1, source_target_pairs={{0,8},{8,0},{16,24},{24,16},{1,9},{9,1},{17,25},{25,17},{2,10},{10... | collective-permute-start | bytes 245768 | tf_op jit(solution)/shard_map/ppermute | solution.py:248
  15.0 5.6 %collective-permute-start.5 = (bf16[2,20,16,128]{3,2,1,0:T(8,128)(2,1)S(1)}, bf16[2,20,16,128]{3,2,1,0:T(8,128)(2,1)S(1)}, u32[]{:S(2)}, u32[]{:S(2)}) collective-permute-start(bf16[2,20,16,128]{3,2,1,0:T(8,128)(2,1)S(1)} %pad_maximum_fusion.1), channel_id=1, source_target_pairs={{0,4},{1,5},{2,6},{3,7},{4,0},{5,1},{6,2},{7,3},{8,12},{9,13},{10,... | collective-permute-start | bytes 491528 | tf_op jit(solution)/shard_map/ppermute | solution.py:59
  17.9 5.4 %collective-permute-start.8 = (bf16[320,128]{1,0:T(8,128)(2,1)S(1)}, bf16[320,128]{1,0:T(8,128)(2,1)S(1)}, u32[]{:S(2)}, u32[]{:S(2)}) collective-permute-start(bf16[320,128]{1,0:T(8,128)(2,1)S(1)} %convert_add_fusion), channel_id=1, source_target_pairs={{0,16},{8,24},{16,0},{24,8},{1,17},{9,25},{17,1},{25,9},{2,18},{10... | collective-permute-start | bytes 245768 | tf_op jit(solution)/shard_map/ppermute | solution.py:248
  20.6 6.3 %collective-permute-start.7 = (bf16[4,20,16,128]{3,2,1,0:T(8,128)(2,1)S(1)}, bf16[4,20,16,128]{3,2,1,0:T(8,128)(2,1)S(1)}, u32[]{:S(2)}, u32[]{:S(2)}) collective-permute-start(bf16[4,20,16,128]{3,2,1,0:T(8,128)(2,1)S(1)} %constant_dynamic-update-slice_fusion.rest_0_), channel_id=1, source_target_pairs={{0,1},{1,0},{2,3},{3,2},{4,5},{5,4},{6,7},{7,6},{8,9},{9,8},{10,11... | collective-permute-start | bytes 983048 | tf_op jit(solution)/shard_map/ppermute | solution.py:50
  23.4 5.4 %collective-permute-start.11 = (bf16[320,128]{1,0:T(8,128)(2,1)S(1)}, bf16[320,128]{1,0:T(8,128)(2,1)S(1)}, u32[]{:S(2)}, u32[]{:S(2)}) collective-permute-start(bf16[320,128]{1,0:T(8,128)(2,1)S(1)} %fusion.2), channel_id=1, source_target_pairs={{0,6},{1,7},{2,4},{3,5},{4,2},{5,3},{6,0},{7,1},{8,14},{9,15},{10,... | collective-permute-start | bytes 245768 | tf_op jit(solution)/shard_map/ppermute | solution.py:59
  25.3 4.4 %collective-permute-start.10 = (bf16[320,128]{1,0:T(8,128)(2,1)S(1)}, bf16[320,128]{1,0:T(8,128)(2,1)S(1)}, u32[]{:S(2)}, u32[]{:S(2)}) collective-permute-start(bf16[320,128]{1,0:T(8,128)(2,1)S(1)} %fusion.2), channel_id=1, source_target_pairs={{0,4},{1,5},{2,6},{3,7},{4,0},{5,1},{6,2},{7,3},{8,12},{9,13},{10,... | collective-permute-start | bytes 245768 | tf_op jit(solution)/shard_map/ppermute | solution.py:59
  25.8 4.4 %collective-permute-start.9 = (bf16[320,128]{1,0:T(8,128)(2,1)S(1)}, bf16[320,128]{1,0:T(8,128)(2,1)S(1)}, u32[]{:S(2)}, u32[]{:S(2)}) collective-permute-start(bf16[320,128]{1,0:T(8,128)(2,1)S(1)} %fusion.2), channel_id=1, source_target_pairs={{0,2},{1,3},{2,0},{3,1},{4,6},{5,7},{6,4},{7,5},{8,10},{9,11},{10,... | collective-permute-start | bytes 245768 | tf_op jit(solution)/shard_map/ppermute | solution.py:59
  26.9 3.5 %copy-start.3 = (bf16[128,2560]{1,0:T(8,128)(2,1)S(1)}, bf16[128,2560]{1,0:T(8,128)(2,1)}, u32[]{:S(2)}) copy-start(bf16[128,2560]{1,0:T(8,128)(2,1)} %v_ref.3) | copy-start | bytes 1966084
  28.5 1.9 %copy-start.2 = (bf16[128,2560]{1,0:T(8,128)(2,1)S(1)}, bf16[128,2560]{1,0:T(8,128)(2,1)}, u32[]{:S(2)}) copy-start(bf16[128,2560]{1,0:T(8,128)(2,1)} %k_ref.3) | copy-start | bytes 1966084
  30.3 1.7 %collective-permute-start.12 = (bf16[4,320,128]{2,1,0:T(8,128)(2,1)S(1)}, bf16[4,320,128]{2,1,0:T(8,128)(2,1)S(1)}, u32[]{:S(2)}, u32[]{:S(2)}) collective-permute-start(bf16[4,320,128]{2,1,0:T(8,128)(2,1)S(1)} %pad_maximum_fusion.state_ref), channel_id=1, source_target_pairs={{0,1},{1,0},{2,3},{3,2},{4,5},{5,4},{6,7},{7,6},{8,9},{9,8},{10,11... | collective-permute-start | bytes 983048 | tf_op jit(solution)/shard_map/ppermute | solution.py:50
